TPU v7x, 512 devices: a whole 4x4x16 slice. The times are simulated.
512 devices in a mesh: ka: 8 (over x, core), pts: 64 (over z, y).
Axes of the slice: x: 4, y: 4, z: 16, core: 2. Of those that a mesh axis runs over, the one named last changes fastest.
Arguments:
- orbitals: bfloat16 [216, 2, 4096, 384], P('ka', None, 'pts'), may hold values from -1.5 to 1.5
- counts: int32 [216], P('ka'), may hold values from 60 to 300
- occupation: float32 [216, 384], P('ka'), may hold values from 0.2 to 1
- coulomb: bfloat16 [216, 2, 64, 4096], P('ka', None, None, 'pts'), may hold values from -24 to 24
Outputs:
- exchange_block: bfloat16 [216, 2, 64, 4096], P('ka', None, None, 'pts')
Inputs may be any that keep to these rules, and one draw needn't show every extreme that they name: `counts`: between 60 and 300 occupied bands per k-point.
All inputs are finite; a program needn't handle non-finite values.
Results may differ from a plain program's by a relative error of at most 0.0057.
Values may be sent and summed in bfloat16 or wider, within the bound.
A program may use at most 64 MiB of HBM per device.

v0:
```python
import jax
import jax.numpy as jnp
from jax import lax
from jax.sharding import Mesh
from jax.sharding import PartitionSpec as P

KSIDE = 6
ROW_DEV = 1
PTS = ("pts_0", "pts_1")
KA = ("ka_0", "ka_1")


def gather_axes(array, axes, dim):
    for axis in reversed(axes):
        array = lax.all_gather(array, axis, axis=dim, tiled=True)
    return array


def split_up(array, dim, devices):
    before, after = (array.shape[:dim], array.shape[dim + 1 :])
    return jnp.moveaxis(array.reshape(*before, devices, -1, *after), dim, 0)


def in_order(parts, dim):
    parts = jnp.moveaxis(parts, 0, dim)
    dims = parts.shape
    return parts.reshape(*dims[:dim], dims[dim] * dims[dim + 1], *dims[dim + 2 :])


def moved_by_axis(parts, axes, turns):
    inside = parts.shape[1:]
    whole = parts.reshape(*(lax.axis_size(a) for a in axes), *inside)
    for k in turns:
        whole = lax.all_to_all(whole, axes[k], k, k, tiled=True)
    return whole.reshape(-1, *inside)


def exchange_by_axis(array, axes, turns, split_dim, concat_dim):
    parts = split_up(array, split_dim, lax.axis_size(axes))
    return in_order(moved_by_axis(parts, axes, turns), concat_dim)


def band_gram(left, right):

    def product(first, second):
        return jnp.einsum("krb,knb->krn", first, second, preferred_element_type=jnp.float32)

    real = product(left[:, 0], right[:, 0]) + product(left[:, 1], right[:, 1])
    imag = product(left[:, 1], right[:, 0]) - product(left[:, 0], right[:, 1])
    return jnp.stack([real, imag], 1)


def side_table(sign):
    index = jnp.arange(KSIDE, dtype=jnp.int32)
    phase = index[:, None] * index[None, :] % KSIDE
    angle = phase.astype(jnp.float32) * (2.0 * jnp.pi / KSIDE)
    cosine = jnp.cos(angle)
    sine = jnp.sin(angle) * sign
    top = jnp.stack([cosine, sine], 2)
    bottom = jnp.stack([-sine, cosine], 2)
    return jnp.stack([top, bottom], 1)


def mesh_transform(values, sign):
    table = side_table(sign)
    forms = ["acbd,bxydm->axycm", "acbd,xbydm->xaycm", "acbd,xybdm->xyacm"]
    for form in forms:
        values = jnp.einsum(
            form, table, values, precision=lax.Precision.HIGHEST, preferred_element_type=jnp.float32
        )
    return values


def convolve(density, kernel):
    shape = density.shape
    count = shape[0]
    dens = mesh_transform(density.astype(jnp.float32).reshape(KSIDE, KSIDE, KSIDE, 2, -1), 1.0)
    kern = mesh_transform(kernel.astype(jnp.float32).reshape(KSIDE, KSIDE, KSIDE, 2, -1), 1.0)
    prod_re = kern[:, :, :, 0] * dens[:, :, :, 0] - kern[:, :, :, 1] * dens[:, :, :, 1]
    prod_im = kern[:, :, :, 0] * dens[:, :, :, 1] + kern[:, :, :, 1] * dens[:, :, :, 0]
    back = mesh_transform(jnp.stack([prod_re, prod_im], 3), -1.0)
    scale = -1.0 / (count * count)
    return (back * scale).reshape(shape).astype(jnp.bfloat16)


def local(orbitals, counts, occupation, coulomb):
    slots = orbitals.shape[3]
    band = jnp.arange(slots, dtype=jnp.int32)
    weights = jnp.where(band[None, :] < counts[:, None], occupation, jnp.float32(0.0))
    weighted = (orbitals[:, :, :ROW_DEV, :].astype(jnp.float32) * weights[:, None, None, :]).astype(
        jnp.bfloat16
    )
    gathered = gather_axes(weighted, PTS, 2)
    density = band_gram(gathered, orbitals).astype(jnp.bfloat16)
    result = convolve(
        lax.all_to_all(density, KA, split_axis=3, concat_axis=0, tiled=True),
        lax.all_to_all(coulomb, KA, split_axis=3, concat_axis=0, tiled=True),
    )
    return exchange_by_axis(result, KA, (1, 0), 0, 3)


def solution(mesh):
    finer = Mesh(mesh.devices.reshape(4, 2, 16, 4), ("ka_0", "ka_1", "pts_0", "pts_1"))
    in_specs = (P(KA, None, PTS, None), P(KA), P(KA, None), P(KA, None, None, PTS))
    out_specs = P(KA, None, None, PTS)
    return jax.shard_map(local, mesh=finer, in_specs=in_specs, out_specs=out_specs, check_vma=False)
```

profile of v0, /device:TPU:1, one launch (start us, length us, event | category | flops | bytes accessed | tf_op | source)
XLA Modules:
  0.0 193.9 jit_solution(1851961340840522494)
XLA Ops:
  6.5 0.0 all-gather.2.cloned.1.call-start
  6.5 1.0 slice.36
  7.6 0.9 fusion.43
  8.4 0.1 multiply_convert_fusion
  8.5 11.3 %all_gather.6 = bf16[27,2,4,384]{3,1,0,2:T(2,128)(2,1)} all-gather(bf16[27,2,1,384]{3,1,0,2:T(2,128)(2,1)S(1)} %multiply_convert_fusion), channel_id=1, replica_groups=mesh['ka_0'=4,'ka_1'=2,'pts_0'=16,'pts_1'=4] {'pts_1'}, dimensions={2}, use_global_device_ids=true | all-gather | bytes 207360 | tf_op jit(solution)/shard_map/all_gather | solution.py:15
  19.8 0.0 all-gather.2.cloned.1.call-update
  19.8 2.4 %copy.57 = bf16[27,2,64,64]{2,1,0,3:T(2,128)(2,1)S(1)} copy(bf16[27,2,64,64]{3,2,1,0:T(8,128)(2,1)} %param.7) | data formatting | bytes 884736 | tf_op args[3]
  22.2 1.3 reshape.130
  23.5 11.8 %all-to-all-start = ((bf16[8,2,13824]{2,1,0:T(2,128)(2,1)}), bf16[8,2,13824]{2,1,0:T(2,128)(2,1)S(1)}, u32[]{:S(2)}, u32[]{:S(2)}) async-start(bf16[8,2,13824]{2,1,0:T(2,128)(2,1)} %reshape.130), calls=%async_computation | async-start | bytes 884736 | tf_op jit(solution)/shard_map/all_to_all | solution.py:97
  35.3 0.1 fusion.59
  35.4 0.1 broadcast_multiply_fusion
  35.5 0.1 fusion.57
  35.7 8.2 %all-to-all-done = bf16[8,2,13824]{2,1,0:T(2,128)(2,1)S(1)} async-done(((bf16[8,2,13824]{2,1,0:T(2,128)(2,1)}), bf16[8,2,13824]{2,1,0:T(2,128)(2,1)S(1)}, u32[]{:S(2)}, u32[]{:S(2)}) %all-to-all-start) | async-done | bytes 442400 | tf_op jit(solution)/shard_map/all_to_all | solution.py:97
  43.9 0.5 reshape.131
  44.5 0.2 copy.158
  44.7 4.8 %copy.59 = bf16[8,27,2,64,8]{4,3,2,1,0:T(8,128)(2,1)} copy(bf16[8,27,2,64,8]{3,4,0,2,1:T(8,128)(2,1)S(1)} %bitcast.175) | data formatting | bytes 884736 | tf_op jit(solution)/shard_map/all_to_all | solution.py:97
  49.5 9.7 %reshape.104 = bf16[6,6,6,2,512]{4,3,2,1,0:T(2,128)(2,1)S(1)} reshape(bf16[8,27,2,64,8]{4,3,2,1,0:T(8,128)(2,1)} %copy.59) | data formatting | bytes 884736 | tf_op jit(solution)/shard_map/reshape | solution.py:78
  59.2 1.1 convolution_bitcast_fusion.8
  60.3 32.4 %all-gather.2.cloned.1.call-done = bf16[27,2,64,384]{3,1,0,2:T(2,128)(2,1)} async-done(((bf16[27,2,4,384]{3,1,0,2:T(2,128)(2,1)}), bf16[27,2,64,384]{3,1,0,2:T(2,128)(2,1)}) %all-gather.2.cloned.1.call-update) | async-done | bytes 2654224 | tf_op jit(solution)/shard_map/all_gather | solution.py:15
  92.7 0.0 copy-start
  92.7 6.9 %fusion.63 = (bf16[27,1,64,384]{3,1,0,2:T(2,128)(2,1)S(1)}, bf16[27,1,64,384]{3,1,0,2:T(2,128)(2,1)S(1)}) fusion(bf16[27,2,64,384]{3,1,0,2:T(2,128)(2,1)} %all-gather.2.cloned.1.call-done), kind=kLoop, calls=%fused_computation.79 | loop fusion | bytes 5308416 | tf_op jit(solution)/shard_map/slice | solution.py:48
  99.7 0.0 copy-done
  99.7 0.6 fusion.3
  100.3 0.6 fusion.1
  100.9 0.6 fusion.23
  101.5 0.6 fusion.26
  102.1 0.2 pad_maximum_fusion
  102.3 0.8 copy.68
  103.1 1.3 reshape.128
  104.4 14.1 %all-to-all-start.1 = ((bf16[8,2,13824]{2,1,0:T(2,128)(2,1)}), bf16[8,2,13824]{2,1,0:T(2,128)(2,1)S(1)}, u32[]{:S(2)}, u32[]{:S(2)}) async-start(bf16[8,2,13824]{2,1,0:T(2,128)(2,1)} %reshape.128), calls=%async_computation.1 | async-start | bytes 884736 | tf_op jit(solution)/shard_map/all_to_all | solution.py:96
  118.5 1.9 convolution_bitcast_fusion.6
  120.5 1.8 convolution_bitcast_fusion.5
  122.2 4.9 %all-to-all-done.1 = bf16[8,2,13824]{2,1,0:T(2,128)(2,1)S(1)} async-done(((bf16[8,2,13824]{2,1,0:T(2,128)(2,1)}), bf16[8,2,13824]{2,1,0:T(2,128)(2,1)S(1)}, u32[]{:S(2)}, u32[]{:S(2)}) %all-to-all-start.1) | async-done | bytes 442400 | tf_op jit(solution)/shard_map/all_to_all | solution.py:96
  127.1 0.5 reshape.129
  127.7 0.2 copy.157
  127.9 4.8 %copy.70 = bf16[8,27,2,64,8]{4,3,2,1,0:T(8,128)(2,1)} copy(bf16[8,27,2,64,8]{3,4,0,2,1:T(8,128)(2,1)S(1)} %bitcast.176) | data formatting | bytes 884736 | tf_op jit(solution)/shard_map/all_to_all | solution.py:96
  132.7 9.7 %reshape.105 = bf16[6,6,6,2,512]{4,3,2,1,0:T(2,128)(2,1)S(1)} reshape(bf16[8,27,2,64,8]{4,3,2,1,0:T(8,128)(2,1)} %copy.70) | data formatting | bytes 884736 | tf_op jit(solution)/shard_map/reshape | solution.py:77
  142.4 0.8 convolution_bitcast_fusion.7
  143.2 1.9 convolution_bitcast_fusion.4
  145.1 1.8 convolution_bitcast_fusion.3
  146.9 0.3 multiply_subtract_fusion
  147.2 0.1 maximum_bitcast_fusion
  147.3 1.8 convolution_bitcast_fusion.2
  149.1 1.9 convolution_bitcast_fusion.1
  151.0 1.7 fusion.22
  152.7 0.3 copy.79
  153.0 9.4 %convert_element_type.66 = bf16[4,2,27,2,64,8]{5,4,3,2,1,0:T(8,128)(2,1)} reshape(bf16[6,6,6,2,512]{4,3,2,1,0:T(2,128)(2,1)S(1)} %copy.79) | data formatting | bytes 884736 | tf_op jit(solution)/shard_map/convert_element_type | solution.py:83
  162.4 5.5 %copy.80 = bf16[4,2,27,2,64,8]{4,5,3,2,0,1:T(8,128)(2,1)S(1)} copy(bf16[4,2,27,2,64,8]{5,4,3,2,1,0:T(8,128)(2,1)} %convert_element_type.66) | data formatting | bytes 884736 | tf_op jit(solution)/shard_map/convert_element_type | solution.py:83
  168.0 0.8 reshape.132
  168.7 4.6 %all_to_all.40 = bf16[2,2,55296]{2,1,0:T(2,128)(2,1)S(1)} all-to-all(bf16[2,2,55296]{2,1,0:T(2,128)(2,1)S(1)} %reshape.132), channel_id=1, replica_groups=mesh['ka_0'=4,'ka_1'=2,'pts_0'=16,'pts_1'=4] {'ka_1'}, dimensions={0} | all-to-all | bytes 884736 | tf_op jit(solution)/shard_map/all_to_all | solution.py:34
  173.3 0.7 reshape.133
  174.0 0.2 copy_bitcast_fusion.8
  174.1 0.5 reshape.134
  174.6 10.4 %all_to_all.41 = bf16[4,2,27648]{2,1,0:T(2,128)(2,1)S(1)} all-to-all(bf16[4,2,27648]{2,1,0:T(2,128)(2,1)S(1)} %reshape.134), channel_id=1, replica_groups=mesh['ka_0'=4,'ka_1'=2,'pts_0'=16,'pts_1'=4] {'ka_0'}, dimensions={0} | all-to-all | bytes 884736 | tf_op jit(solution)/shard_map/all_to_all | solution.py:34
  185.1 0.5 reshape.135
  185.6 0.2 copy.82
  185.8 1.2 copy.83
  (5 shorter events, 0.0 us)
Async XLA Ops:
  6.5 86.2 %all-gather.2.cloned.1.call-start = ((), (), s32[]{:S(2)}) async-start(), calls=%async_computation.4 | async-start | bytes 2820096 | tf_op jit(solution)/shard_map/all_gather | solution.py:15
  23.5 20.4 %all-to-all-start = ((bf16[8,2,13824]{2,1,0:T(2,128)(2,1)}), bf16[8,2,13824]{2,1,0:T(2,128)(2,1)S(1)}, u32[]{:S(2)}, u32[]{:S(2)}) async-start(bf16[8,2,13824]{2,1,0:T(2,128)(2,1)} %reshape.130), calls=%async_computation | async-start | bytes 884736 | tf_op jit(solution)/shard_map/all_to_all | solution.py:97
  92.7 6.9 %copy-start = (bf16[27,2,64,384]{3,2,1,0:T(8,128)(2,1)S(1)}, bf16[27,2,64,384]{3,2,1,0:T(8,128)(2,1)}, u32[]{:S(2)}) copy-start(bf16[27,2,64,384]{3,2,1,0:T(8,128)(2,1)} %param.4) | copy-start | bytes 7962628
  104.4 22.7 %all-to-all-start.1 = ((bf16[8,2,13824]{2,1,0:T(2,128)(2,1)}), bf16[8,2,13824]{2,1,0:T(2,128)(2,1)S(1)}, u32[]{:S(2)}, u32[]{:S(2)}) async-start(bf16[8,2,13824]{2,1,0:T(2,128)(2,1)} %reshape.128), calls=%async_computation.1 | async-start | bytes 884736 | tf_op jit(solution)/shard_map/all_to_all | solution.py:96
Sparse Core Ops, SparseCore 0:
  19.9 72.7 all-gather.1
where the time goes:
time: 195 us; the launch traced here: 194 us
  local copies, waits for them, and re-layouts  63.6 us (33%)
  waiting for transfers between devices  45.5 us (23%)
  blocking collectives  26.3 us (13%)
  starting transfers between devices  25.9 us (13%)
  matrix products  17.1 us (9%)
  between operations  13.7 us (7%)
    all_gather x1, waiting for transfers between devices, gather_axes(): array = lax.all_gather(array, axis, axis=dim, tiled=True)  32.4 us
    convert_element_type x3, local copies, waits for them, and re-layouts, convolve(): return (back * scale).reshape(shape).astype(jnp.bfloat16)  15.3 us
    all_to_all x2, blocking collectives, moved_by_axis(): whole = lax.all_to_all(whole, axes[k], k, k, tiled=True)  15 us
    dot_general x9, matrix products, mesh_transform(): jnp.einsum(form, table, values, precision=lax.Precision.HIGHEST, preferre...  14.7 us
    all_to_all x1, starting transfers between devices, local(): lax.all_to_all(density, KA, split_axis=3, concat_axis=0, tiled=True)  14.1 us
    all_to_all x1, starting transfers between devices, local(): lax.all_to_all(coulomb, KA, split_axis=3, concat_axis=0, tiled=True)  11.8 us
    all_gather x1, blocking collectives, gather_axes(): array = lax.all_gather(array, axis, axis=dim, tiled=True)  11.3 us
    reshape x1, local copies, waits for them, and re-layouts, convolve(): kernel.astype(jnp.float32).reshape(KSIDE, KSIDE, KSIDE, 2, -1)  9.7 us
  transfers between devices with their start and end apart: 3, of which 3 were waited for; matrix products, arithmetic and copies ran while one was open for 12% of the time, Pallas kernels for 0%

commit v1 on v0

--- a/solution.py
+++ b/solution.py
@@ -94,7 +94,10 @@
     density = band_gram(gathered, orbitals).astype(jnp.bfloat16)
     result = convolve(
         lax.all_to_all(density, KA, split_axis=3, concat_axis=0, tiled=True),
-        lax.all_to_all(coulomb, KA, split_axis=3, concat_axis=0, tiled=True),
+        jnp.concatenate(
+            lax.all_to_all(jnp.stack(jnp.split(coulomb, lax.axis_size(KA), axis=3)), KA, 0, 0),
+            axis=0,
+        ),
     )
     return exchange_by_axis(result, KA, (1, 0), 0, 3)
 

time: 195 us -> 195 us (level)
  local copies, waits for them, and re-layouts: 63.6 us -> 80.7 us
  waiting for transfers between devices: 45.5 us -> 29.2 us
    all_gather x1, waiting for transfers between devices: 32.4 us -> 16 us  [gather_axes(): array = lax.all_gather(array, axis, axis=dim, tiled=True)]
    unnamed x13 -> x36, local copies, waits for them, and re-layouts: 8.7 us -> 17.3 us
    split x0 -> x1, local copies, waits for them, and re-layouts: none -> 8.48 us  [local(): jnp.split(coulomb, lax.axis_size(KA), axis=3)]
    all_to_all x2 -> x1, local copies, waits for them, and re-layouts: 5.02 us -> 4.82 us  [local(): lax.all_to_all(jnp.stack(jnp.split(coulomb, lax.axis_size(KA), axis=3)),...]
  transfers between devices with their start and end apart: 3 -> 3, of which waited for: 3 -> 3; matrix products, arithmetic and copies ran while one was open for 12% -> 21% of each run, Pallas kernels for 0% -> 0%
where the time goes in v1:
time: 195 us; the launch traced here: 194 us
  local copies, waits for them, and re-layouts  80.7 us (41%)
  waiting for transfers between devices  29.2 us (15%)
  blocking collectives  26.3 us (13%)
  starting transfers between devices  25.6 us (13%)
  matrix products  16.7 us (9%)
  between operations  13.8 us (7%)
    unnamed x36, local copies, waits for them, and re-layouts  17.3 us
    all_gather x1, waiting for transfers between devices, gather_axes(): array = lax.all_gather(array, axis, axis=dim, tiled=True)  16 us
    convert_element_type x3, local copies, waits for them, and re-layouts, convolve(): return (back * scale).reshape(shape).astype(jnp.bfloat16)  15.2 us
    all_to_all x2, blocking collectives, moved_by_axis(): whole = lax.all_to_all(whole, axes[k], k, k, tiled=True)  15 us
    dot_general x9, matrix products, mesh_transform(): jnp.einsum(form, table, values, precision=lax.Precision.HIGHEST, preferre...  14.2 us
    all_to_all x1, starting transfers between devices, local(): lax.all_to_all(density, KA, split_axis=3, concat_axis=0, tiled=True)  13.8 us
    all_to_all x1, starting transfers between devices, local(): lax.all_to_all(jnp.stack(jnp.split(coulomb, lax.axis_size(KA), axis=3)),...  11.8 us
    all_gather x1, blocking collectives, gather_axes(): array = lax.all_gather(array, axis, axis=dim, tiled=True)  11.3 us
  transfers between devices with their start and end apart: 3, of which 3 were waited for; matrix products, arithmetic and copies ran while one was open for 21% of the time, Pallas kernels for 0%

profile of v1, /device:TPU:1, one launch (start us, length us, event | category | flops | bytes accessed | tf_op | source)
XLA Modules:
  0.0 194.1 jit_solution(13398385323474761805)
XLA Ops:
  6.5 1.0 slice.36
  7.6 0.9 fusion.42
  8.4 0.1 multiply_convert_fusion
  8.5 11.3 %all_gather.6 = bf16[27,2,4,384]{3,1,0,2:T(2,128)(2,1)} all-gather(bf16[27,2,1,384]{3,1,0,2:T(2,128)(2,1)S(1)} %multiply_convert_fusion), channel_id=1, replica_groups=mesh['ka_0'=4,'ka_1'=2,'pts_0'=16,'pts_1'=4] {'pts_1'}, dimensions={2}, use_global_device_ids=true | all-gather | bytes 207360 | tf_op jit(solution)/shard_map/all_gather | solution.py:15
  19.8 8.5 %fusion.63 = (bf16[27,2,64,8]{3,2,1,0:T(8,128)(2,1)S(1)}, bf16[27,2,64,8]{3,2,1,0:T(8,128)(2,1)S(1)}, bf16[27,2,64,8]{3,2,1,0:T(8,128)(2,1)S(1)}, bf16[27,2,64,8...) fusion(bf16[27,2,64,64]{3,2,1,0:T(8,128)(2,1)} %param.7), kind=kLoop, calls=%fused_computation.85 | loop fusion | bytes 884736 | tf_op jit(solution)/shard_map/split | solution.py:98
  28.3 2.1 %copy.132 = bf16[27,2,64,8]{2,3,1,0:T(8,128)(2,1)} copy(bf16[27,2,64,8]{3,2,1,0:T(8,128)(2,1)} %get-tuple-element.16) | data formatting | bytes 110592
  30.4 2.1 %copy.133 = bf16[27,2,64,8]{2,3,1,0:T(8,128)(2,1)} copy(bf16[27,2,64,8]{3,2,1,0:T(8,128)(2,1)} %get-tuple-element.15) | data formatting | bytes 110592
  32.5 2.1 %copy.134 = bf16[27,2,64,8]{2,3,1,0:T(8,128)(2,1)} copy(bf16[27,2,64,8]{3,2,1,0:T(8,128)(2,1)} %get-tuple-element.14) | data formatting | bytes 110592
  34.6 2.1 %copy.135 = bf16[27,2,64,8]{2,3,1,0:T(8,128)(2,1)} copy(bf16[27,2,64,8]{3,2,1,0:T(8,128)(2,1)} %get-tuple-element.13) | data formatting | bytes 110592
  36.7 0.9 copy.136
  37.6 0.3 copy.137
  38.0 0.3 copy.138
  38.3 0.3 copy.139
  38.6 0.2 copy-done.3
  38.9 0.0 copy-done.4
  38.9 0.0 copy-done.2
  39.0 0.2 copy-done
  39.3 1.3 reshape.131
  40.7 11.8 %all-to-all-start = ((bf16[8,2,13824]{2,1,0:T(2,128)(2,1)}), bf16[8,2,13824]{2,1,0:T(2,128)(2,1)S(1)}, u32[]{:S(2)}, u32[]{:S(2)}) async-start(bf16[8,2,13824]{2,1,0:T(2,128)(2,1)} %reshape.131), calls=%async_computation | async-start | bytes 884736 | tf_op jit(solution)/shard_map/all_to_all | solution.py:98
  52.4 0.1 fusion.52
  52.5 0.1 fusion.50
  52.7 0.1 broadcast_multiply_fusion
  52.8 8.2 %all-to-all-done = bf16[8,2,13824]{2,1,0:T(2,128)(2,1)S(1)} async-done(((bf16[8,2,13824]{2,1,0:T(2,128)(2,1)}), bf16[8,2,13824]{2,1,0:T(2,128)(2,1)S(1)}, u32[]{:S(2)}, u32[]{:S(2)}) %all-to-all-start) | async-done | bytes 442400 | tf_op jit(solution)/shard_map/all_to_all | solution.py:98
  61.1 0.5 reshape.132
  61.6 4.8 %copy.67 = bf16[8,27,2,64,8]{4,3,2,1,0:T(8,128)(2,1)} copy(bf16[8,27,2,64,8]{3,4,2,1,0:T(8,128)(2,1)S(1)} %bitcast.176) | data formatting | bytes 884736 | tf_op jit(solution)/shard_map/all_to_all | solution.py:98
  66.4 9.7 %reshape.105 = bf16[6,6,6,2,512]{4,3,2,1,0:T(2,128)(2,1)S(1)} reshape(bf16[8,27,2,64,8]{4,3,2,1,0:T(8,128)(2,1)} %copy.67) | data formatting | bytes 884736 | tf_op jit(solution)/shard_map/reshape | solution.py:78
  76.2 0.8 convolution_bitcast_fusion.8
  77.0 16.0 %all-gather.2.cloned.1.call-done = bf16[27,2,64,384]{3,1,0,2:T(2,128)(2,1)} async-done(((bf16[27,2,4,384]{3,1,0,2:T(2,128)(2,1)}), bf16[27,2,64,384]{3,1,0,2:T(2,128)(2,1)}) %all-gather.2.cloned.1.call-update) | async-done | bytes 2654224 | tf_op jit(solution)/shard_map/all_gather | solution.py:15
  93.0 6.9 %fusion.62 = (bf16[27,1,64,384]{3,1,0,2:T(2,128)(2,1)S(1)}, bf16[27,1,64,384]{3,1,0,2:T(2,128)(2,1)S(1)}) fusion(bf16[27,2,64,384]{3,1,0,2:T(2,128)(2,1)} %all-gather.2.cloned.1.call-done), kind=kLoop, calls=%fused_computation.84 | loop fusion | bytes 5308416 | tf_op jit(solution)/shard_map/slice | solution.py:48
  99.9 0.6 fusion.1
  100.5 0.6 fusion.3
  101.1 0.6 fusion.26
  101.8 0.6 fusion.23
  102.4 0.2 pad_maximum_fusion
  102.6 0.8 copy.78
  103.4 1.3 reshape.129
  104.7 13.8 %all-to-all-start.1 = ((bf16[8,2,13824]{2,1,0:T(2,128)(2,1)}), bf16[8,2,13824]{2,1,0:T(2,128)(2,1)S(1)}, u32[]{:S(2)}, u32[]{:S(2)}) async-start(bf16[8,2,13824]{2,1,0:T(2,128)(2,1)} %reshape.129), calls=%async_computation.1 | async-start | bytes 884736 | tf_op jit(solution)/shard_map/all_to_all | solution.py:96
  118.5 1.9 convolution_bitcast_fusion.6
  120.4 1.8 convolution_bitcast_fusion.5
  122.2 5.0 %all-to-all-done.1 = bf16[8,2,13824]{2,1,0:T(2,128)(2,1)S(1)} async-done(((bf16[8,2,13824]{2,1,0:T(2,128)(2,1)}), bf16[8,2,13824]{2,1,0:T(2,128)(2,1)S(1)}, u32[]{:S(2)}, u32[]{:S(2)}) %all-to-all-start.1) | async-done | bytes 442400 | tf_op jit(solution)/shard_map/all_to_all | solution.py:96
  127.1 0.5 reshape.130
  127.7 0.2 copy.172
  127.9 4.8 %copy.80 = bf16[8,27,2,64,8]{4,3,2,1,0:T(8,128)(2,1)} copy(bf16[8,27,2,64,8]{3,4,0,2,1:T(8,128)(2,1)S(1)} %bitcast.175) | data formatting | bytes 884736 | tf_op jit(solution)/shard_map/all_to_all | solution.py:96
  132.7 9.9 %reshape.106 = bf16[6,6,6,2,512]{4,3,2,1,0:T(2,128)(2,1)S(1)} reshape(bf16[8,27,2,64,8]{4,3,2,1,0:T(8,128)(2,1)} %copy.80) | data formatting | bytes 884736 | tf_op jit(solution)/shard_map/reshape | solution.py:77
  142.6 0.8 convolution_bitcast_fusion.7
  143.5 1.9 convolution_bitcast_fusion.4
  145.3 1.8 convolution_bitcast_fusion.3
  147.1 0.3 multiply_subtract_fusion
  147.4 0.1 maximum_bitcast_fusion
  147.5 1.8 convolution_bitcast_fusion.2
  149.3 1.9 convolution_bitcast_fusion.1
  151.2 1.7 fusion.22
  152.9 0.3 copy.89
  153.3 9.4 %convert_element_type.66 = bf16[4,2,27,2,64,8]{5,4,3,2,1,0:T(8,128)(2,1)} reshape(bf16[6,6,6,2,512]{4,3,2,1,0:T(2,128)(2,1)S(1)} %copy.89) | data formatting | bytes 884736 | tf_op jit(solution)/shard_map/convert_element_type | solution.py:83
  162.6 5.5 %copy.90 = bf16[4,2,27,2,64,8]{4,5,3,2,0,1:T(8,128)(2,1)S(1)} copy(bf16[4,2,27,2,64,8]{5,4,3,2,1,0:T(8,128)(2,1)} %convert_element_type.66) | data formatting | bytes 884736 | tf_op jit(solution)/shard_map/convert_element_type | solution.py:83
  168.1 0.8 reshape.133
  168.9 4.6 %all_to_all.30 = bf16[2,2,55296]{2,1,0:T(2,128)(2,1)S(1)} all-to-all(bf16[2,2,55296]{2,1,0:T(2,128)(2,1)S(1)} %reshape.133), channel_id=1, replica_groups=mesh['ka_0'=4,'ka_1'=2,'pts_0'=16,'pts_1'=4] {'ka_1'}, dimensions={0} | all-to-all | bytes 884736 | tf_op jit(solution)/shard_map/all_to_all | solution.py:34
  173.5 0.7 reshape.134
  174.2 0.2 copy_bitcast_fusion.7
  174.3 0.5 reshape.135
  174.8 10.4 %all_to_all.31 = bf16[4,2,27648]{2,1,0:T(2,128)(2,1)S(1)} all-to-all(bf16[4,2,27648]{2,1,0:T(2,128)(2,1)S(1)} %reshape.135), channel_id=1, replica_groups=mesh['ka_0'=4,'ka_1'=2,'pts_0'=16,'pts_1'=4] {'ka_0'}, dimensions={0} | all-to-all | bytes 884736 | tf_op jit(solution)/shard_map/all_to_all | solution.py:34
  185.3 0.5 reshape.136
  185.8 0.2 copy.92
  186.0 1.2 copy.93
  (23 shorter events, 0.2 us)
Async XLA Ops:
  6.5 86.5 %all-gather.2.cloned.1.call-start = ((), (), s32[]{:S(2)}) async-start(), calls=%async_computation.4 | async-start | bytes 2820096 | tf_op jit(solution)/shard_map/all_gather | solution.py:15
  37.9 0.9 copy-start.3
  37.9 1.0 copy-start.4
  38.0 1.0 copy-start.2
  38.0 1.1 copy-start.1
  38.3 1.0 copy-start
  40.7 20.4 %all-to-all-start = ((bf16[8,2,13824]{2,1,0:T(2,128)(2,1)}), bf16[8,2,13824]{2,1,0:T(2,128)(2,1)S(1)}, u32[]{:S(2)}, u32[]{:S(2)}) async-start(bf16[8,2,13824]{2,1,0:T(2,128)(2,1)} %reshape.131), calls=%async_computation | async-start | bytes 884736 | tf_op jit(solution)/shard_map/all_to_all | solution.py:98
  93.0 6.9 %copy-start.5 = (bf16[27,2,64,384]{3,2,1,0:T(8,128)(2,1)S(1)}, bf16[27,2,64,384]{3,2,1,0:T(8,128)(2,1)}, u32[]{:S(2)}) copy-start(bf16[27,2,64,384]{3,2,1,0:T(8,128)(2,1)} %param.4) | copy-start | bytes 7962628
  104.7 22.4 %all-to-all-start.1 = ((bf16[8,2,13824]{2,1,0:T(2,128)(2,1)}), bf16[8,2,13824]{2,1,0:T(2,128)(2,1)S(1)}, u32[]{:S(2)}, u32[]{:S(2)}) async-start(bf16[8,2,13824]{2,1,0:T(2,128)(2,1)} %reshape.129), calls=%async_computation.1 | async-start | bytes 884736 | tf_op jit(solution)/shard_map/all_to_all | solution.py:96
Sparse Core Ops, SparseCore 0:
  19.9 73.0 all-gather.1
